TPU v7x, 256 devices: a whole 4x4x8 slice. The times are simulated.
256 devices in a mesh: ex: 8 (over z), ey: 16 (over y, x), tp: 2 (over core).
Axes of the slice: x: 4, y: 4, z: 8, core: 2. Of those that a mesh axis runs over, the one named last changes fastest.
Arguments:
- layer_input: bfloat16 [8192, 4096], P(('ex', 'ey'), 'tp'), may hold values from -6 to 6
- out_grad: bfloat16 [8192, 4096], P(('ex', 'ey'), 'tp'), may hold values from -6 to 6
- gate_prob: bfloat16 [8192, 8], P(('ex', 'ey')), may hold values from 0.099609375 to 1
- expert_ids: int32 [8192, 8], P(('ex', 'ey')), may hold values from 0 to 127, all different within a row; in each aligned block of 64 rows (0 to 63, 64 to 127, ...) at most 6 rows name the same one
- gate_weight: bfloat16 [128, 4096, 768], P(('ex', 'ey'), None, 'tp'), may hold values from -0.09375 to 0.09375
- up_weight: bfloat16 [128, 4096, 768], P(('ex', 'ey'), None, 'tp'), may hold values from -0.09375 to 0.09375
- down_weight: bfloat16 [128, 768, 4096], P(('ex', 'ey'), 'tp'), may hold values from -0.21875 to 0.21875
Outputs:
- input_grad: bfloat16 [8192, 4096], P(('ex', 'ey'), 'tp')
- prob_grad: bfloat16 [8192, 8], P(('ex', 'ey'))
- down_grad: bfloat16 [128, 768, 4096], P(('ex', 'ey'), 'tp')
Inputs may be any that keep to these rules, and one draw needn't show every extreme that they name: `expert_ids`: each row names 8 different experts. In each aligned block of 64 rows (the tokens of one index of ex and ey) no expert is named by more than 6 rows, a bound that some block reaches.
All inputs are finite; a program needn't handle non-finite values.
Results may differ from a plain program's by a relative error of at most 0.0065.
Values may be sent and summed in bfloat16 or wider, within the bound.
No kernel may reach another device: no remote copies, remote signals or barrier semaphores. Data moves between devices by JAX's collectives and lax.ppermute only.
A program may use at most 128 MiB of HBM per device.

v0:
```python
import jax
import jax.numpy as jnp
from jax import lax
from jax.sharding import PartitionSpec as P


def body(layer_input, out_grad, gate_prob, expert_ids, gate_weight, up_weight, down_weight):
    tok_rows, choose = expert_ids.shape
    half_width = layer_input.shape[1]
    local_experts = gate_weight.shape[0]
    cycle_high = lax.axis_size("ex")
    cycle_low = lax.axis_size("ey")
    holders = cycle_high * cycle_low
    experts = holders * local_experts
    capacity = 3 * tok_rows * choose // (2 * experts)
    routes = tok_rows * choose
    total_slots = experts * capacity
    flat_ids = expert_ids.reshape(routes)
    onehot = (flat_ids[:, None] == jnp.arange(experts, dtype=jnp.int32)[None, :]).astype(jnp.int32)
    before = jnp.sum((jnp.cumsum(onehot, axis=0) - onehot) * onehot, axis=1)
    slot_of = flat_ids * capacity + before
    source = (
        jnp.full((total_slots,), routes, jnp.int32)
        .at[slot_of]
        .set(jnp.arange(routes, dtype=jnp.int32))
    )
    filled = source < routes
    route_idx = jnp.minimum(source, routes - 1)
    token_of = route_idx // choose
    send_inputs = jnp.where(
        filled[:, None], layer_input[token_of], jnp.zeros((), layer_input.dtype)
    )
    send_grads = jnp.where(filled[:, None], out_grad[token_of], jnp.zeros((), out_grad.dtype))
    send_probs = jnp.where(
        filled, gate_prob.reshape(routes)[route_idx], jnp.zeros((), gate_prob.dtype)
    )
    recv_inputs, recv_grads, recv_probs = (
        lax.all_to_all(send_inputs, ("ex", "ey"), split_axis=0, concat_axis=0, tiled=True),
        lax.all_to_all(send_grads, ("ex", "ey"), split_axis=0, concat_axis=0, tiled=True),
        lax.all_to_all(send_probs, ("ex", "ey"), split_axis=0, concat_axis=0, tiled=True),
    )
    full_inputs, full_grads = (
        lax.all_gather(recv_inputs, "tp", axis=1, tiled=True),
        lax.all_gather(recv_grads, "tp", axis=1, tiled=True),
    )
    width = full_inputs.shape[1]
    rows_in = full_inputs.reshape(holders, local_experts, capacity, width)
    rows_grad = full_grads.reshape(holders, local_experts, capacity, width)
    route_weight = recv_probs.reshape(holders, local_experts, capacity).astype(jnp.float32)[
        ..., None
    ]
    gate_pre = jnp.einsum(
        "secd,edh->sech", rows_in, gate_weight, preferred_element_type=jnp.float32
    )
    up_pre = jnp.einsum("secd,edh->sech", rows_in, up_weight, preferred_element_type=jnp.float32)
    gate_sigmoid = jax.nn.sigmoid(gate_pre)
    silu_gate = gate_pre * gate_sigmoid
    hidden_act = silu_gate * up_pre
    weighted = (route_weight * hidden_act).astype(jnp.bfloat16)
    down_grad = jnp.einsum(
        "sech,secd->ehd", weighted, rows_grad, preferred_element_type=jnp.float32
    ).astype(jnp.bfloat16)
    hidden_grad = jnp.einsum(
        "secd,ehd->sech", rows_grad, down_weight, preferred_element_type=jnp.float32
    )
    prob_part = jnp.sum(hidden_grad * hidden_act, axis=3)
    prob_total = lax.psum(prob_part, "tp")
    gate_grad = (
        route_weight * hidden_grad * up_pre * gate_sigmoid * (1.0 + gate_pre * (1.0 - gate_sigmoid))
    ).astype(jnp.bfloat16)
    up_grad = (route_weight * hidden_grad * silu_gate).astype(jnp.bfloat16)
    partial_value = jnp.einsum(
        "sech,edh->secd", gate_grad, gate_weight, preferred_element_type=jnp.float32
    )
    partial_value = partial_value + jnp.einsum(
        "sech,edh->secd", up_grad, up_weight, preferred_element_type=jnp.float32
    )
    back_rows = lax.psum_scatter(
        partial_value.reshape(total_slots, width).astype(jnp.bfloat16),
        "tp",
        scatter_dimension=1,
        tiled=True,
    )
    back_probs = prob_total.reshape(total_slots).astype(jnp.bfloat16)
    home_rows, home_probs = (
        lax.all_to_all(back_rows, ("ex", "ey"), split_axis=0, concat_axis=0, tiled=True),
        lax.all_to_all(back_probs, ("ex", "ey"), split_axis=0, concat_axis=0, tiled=True),
    )
    picked = home_rows[slot_of].astype(jnp.float32).reshape(tok_rows, choose, half_width)
    input_grad = jnp.sum(picked, axis=1).astype(jnp.bfloat16)
    prob_grad = home_probs[slot_of].reshape(tok_rows, choose)
    return (input_grad, prob_grad, down_grad)


def solution(mesh):
    return jax.shard_map(
        body,
        mesh=mesh,
        in_specs=(
            P(("ex", "ey"), "tp"),
            P(("ex", "ey"), "tp"),
            P(("ex", "ey"), None),
            P(("ex", "ey"), None),
            P(("ex", "ey"), None, "tp"),
            P(("ex", "ey"), None, "tp"),
            P(("ex", "ey"), "tp", None),
        ),
        out_specs=(P(("ex", "ey"), "tp"), P(("ex", "ey"), None), P(("ex", "ey"), "tp", None)),
        check_vma=False,
    )
```

profile of v0, /device:TPU:32, one launch (start us, length us, event | category | flops | bytes accessed | tf_op | source)
XLA Modules:
  0.0 535.4 jit_solution(8489592237368747575)
XLA Ops:
  12.6 2.4 scatter_custom_fusion
  15.0 5.0 gather_fusion
  20.2 4.2 gather_fusion.2
  24.5 6.3 %gather.25 = bf16[128,6,2048]{2,1,0:T(8,128)(2,1)} reshape(bf16[768,2048]{1,0:T(8,128)(2,1)} %gather_fusion.2) | data formatting | bytes 6291456 | tf_op jit(solution)/shard_map/gather | solution.py:31
  30.8 4.2 gather_fusion.1
  35.0 6.3 %gather.23 = bf16[128,6,2048]{2,1,0:T(8,128)(2,1)} reshape(bf16[768,2048]{1,0:T(8,128)(2,1)} %gather_fusion.1) | data formatting | bytes 6291456 | tf_op jit(solution)/shard_map/gather | solution.py:33
  41.3 5.2 broadcast_select_fusion.1
  46.5 111.1 %all_to_all.49 = bf16[128,6,2048]{2,1,0:T(8,128)(2,1)} all-to-all(bf16[128,6,2048]{2,1,0:T(8,128)(2,1)S(1)} %get-tuple-element.12), channel_id=1, replica_groups=mesh['ex'=8,'ey'=16,'tp'=2] {'ex','ey'}, dimensions={0} | all-to-all | bytes 6291456 | tf_op jit(solution)/shard_map/all_to_all | solution.py:38
  157.6 6.3 %all_to_all.37 = bf16[768,2048]{1,0:T(8,128)(2,1)} reshape(bf16[128,6,2048]{2,1,0:T(8,128)(2,1)} %all_to_all.49) | data formatting | bytes 6291456 | tf_op jit(solution)/shard_map/all_to_all | solution.py:38
  164.0 104.5 %all_to_all.50 = bf16[128,6,2048]{2,1,0:T(8,128)(2,1)} all-to-all(bf16[128,6,2048]{2,1,0:T(8,128)(2,1)} %get-tuple-element.11), channel_id=1, replica_groups=mesh['ex'=8,'ey'=16,'tp'=2] {'ex','ey'}, dimensions={0} | all-to-all | bytes 6291456 | tf_op jit(solution)/shard_map/all_to_all | solution.py:39
  268.5 6.3 %all_to_all.35 = bf16[768,2048]{1,0:T(8,128)(2,1)} reshape(bf16[128,6,2048]{2,1,0:T(8,128)(2,1)} %all_to_all.50) | data formatting | bytes 6291456 | tf_op jit(solution)/shard_map/all_to_all | solution.py:39
  275.0 20.2 %all_to_all.51 = bf16[128,6,1]{1,2,0:T(2,128)(2,1)S(1)} all-to-all(bf16[128,6,1]{1,2,0:T(2,128)(2,1)S(1)} %all_to_all.43), channel_id=1, replica_groups=mesh['ex'=8,'ey'=16,'tp'=2] {'ex','ey'}, dimensions={0} | all-to-all | bytes 3072 | tf_op jit(solution)/shard_map/all_to_all | solution.py:40
  295.3 10.2 %reshape.158 = bf16[128,6,4096]{2,1,0:T(8,128)(2,1)} reshape(bf16[768,4096]{1,0:T(8,128)(2,1)} %all-gather.5.cloned.1.call-done) | data formatting | bytes 12582912 | tf_op jit(solution)/shard_map/reshape.8
  305.5 12.2 %fusion.25 = f32[128,1,6,384]{3,0,2,1:T(8,128)} fusion(bf16[1,4096,384]{2,1,0:T(8,128)(2,1)S(1)} %copy-done, bf16[128,6,4096]{2,1,0:T(8,128)(2,1)} %reshape.158), kind=kOutput, calls=%fused_computation.28 | convolution fusion | flops 2415919104 | bytes 10616832 | tf_op jit(solution)/shard_map/secd,edh->sech/dot_general | solution.py:52
  317.7 7.9 %fusion.20 = f32[128,1,6,384]{3,0,2,1:T(8,128)} fusion(bf16[1,4096,384]{2,1,0:T(8,128)(2,1)S(1)} %copy-done.5, bf16[128,6,4096]{2,1,0:T(8,128)(2,1)S(1)} %copy-done.3), kind=kOutput, calls=%fused_computation.27 | convolution fusion | flops 2415919104 | bytes 10616832 | tf_op jit(solution)/shard_map/secd,edh->sech/dot_general | solution.py:55
  325.6 10.3 %reshape.156 = bf16[128,6,4096]{2,1,0:T(8,128)(2,1)} reshape(bf16[768,4096]{1,0:T(8,128)(2,1)} %all-gather.3.cloned.1.call-done) | data formatting | bytes 12582912 | tf_op jit(solution)/shard_map/reshape.5
  335.9 12.4 %multiply_reduce_fusion = (f32[128,6]{0,1:T(8,128)S(1)}, f32[128,1,6,384]{3,0,2,1:T(8,128)S(1)}) fusion(f32[128,1,6,384]{3,0,2,1:T(8,128)} %fusion.20, f32[128,1,6,384]{3,0,2,1:T(8,128)} %fusion.25, bf16[1,384,4096]{2,1,0:T(8,128)(2,1)} %param.13, bf16[128,6,4096]{2,1,0:T(8,128)(2,1)} %reshape.156), kind=kOutput, calls=%fused_computation.30 | convolution fusion | flops 2417982720 | bytes 12979200 | tf_op jit(solution)/shard_map/secd,ehd->sech/dot_general | solution.py:63
  348.4 6.9 %fusion.9 = f32[128,6,4096]{2,0,1:T(8,128)} fusion(bf16[1,4096,384]{2,1,0:T(8,128)(2,1)S(1)} %copy-done, f32[128,1,6,384]{3,0,2,1:T(8,128)S(1)} %copy-done.4, f32[128,1,6,384]{3,0,2,1:T(8,128)S(1)} %copy-done.6, f32[128,1,6,384]{3,0,2,1:T(8,128)S(1)} %get-tuple-element.16, f32[128,6]{0,1:T(8,128)S(1)} %copy.32), kind=kOutput, calls=%fused_computation.19 | convolution fusion | flops 2419163136 | bytes 19270656 | tf_op jit(solution)/shard_map/sech,edh->secd/dot_general | solution.py:72
  355.3 7.9 %fusion = bf16[128,1,6,4096]{3,0,2,1:T(8,128)(2,1)S(1)} fusion(f32[128,6,4096]{2,0,1:T(8,128)} %fusion.9, bf16[1,4096,384]{2,1,0:T(8,128)(2,1)} %param.12, f32[128,1,6,384]{3,0,2,1:T(8,128)S(1)} %get-tuple-element.16, f32[128,6]{0,1:T(8,128)S(1)} %copy.32, f32[128,1,6,384]{3,0,2,1:T(8,128)S(1)} %copy-done.4), kind=kOutput, calls=%fused_computation.8 | convolution fusion | flops 2424274944 | bytes 24382464 | tf_op jit(solution)/shard_map/sech,edh->secd/dot_general | solution.py:75
  363.2 6.7 %copy.36 = bf16[128,1,6,4096]{3,2,0,1:T(8,128)(2,1)} copy(bf16[128,1,6,4096]{3,0,2,1:T(8,128)(2,1)S(1)} %fusion) | data formatting | bytes 12582912 | tf_op jit(solution)/shard_map/convert_element_type | solution.py:79
  370.0 10.2 %convert_element_type.75 = bf16[768,4096]{1,0:T(8,128)(2,1)} reshape(bf16[128,1,6,4096]{3,2,0,1:T(8,128)(2,1)} %copy.36) | data formatting | bytes 12582912 | tf_op jit(solution)/shard_map/convert_element_type | solution.py:79
  380.2 2.5 psum.7
  383.5 6.6 %all-to-all-start.4 = ((bf16[128,6,1]{1,2,0:T(2,128)(2,1)}), bf16[128,6,1]{1,2,0:T(2,128)(2,1)S(1)}, u32[]{:S(2)}, u32[]{:S(2)}) async-start(bf16[128,6,1]{1,2,0:T(2,128)(2,1)} %copy.37), calls=%async_computation.5 | async-start | bytes 131072 | tf_op jit(solution)/shard_map/all_to_all | solution.py:87
  390.1 3.9 reduce-scatter.2.cloned.1.call-done
  393.9 6.3 %all_to_all.38 = bf16[128,6,2048]{2,1,0:T(8,128)(2,1)} reshape(bf16[768,2048]{1,0:T(8,128)(2,1)} %reduce-scatter.2.cloned.1.call-done) | data formatting | bytes 6291456 | tf_op jit(solution)/shard_map/all_to_all | solution.py:86
  401.4 13.3 %all-to-all-start.3 = ((bf16[128,6,2048]{2,1,0:T(8,128)(2,1)}), bf16[128,6,2048]{2,1,0:T(8,128)(2,1)}, u32[]{:S(2)}, u32[]{:S(2)}) async-start(bf16[128,6,2048]{2,1,0:T(8,128)(2,1)} %all_to_all.38), calls=%async_computation.4 | async-start | bytes 8388608 | tf_op jit(solution)/shard_map/all_to_all | solution.py:86
  414.7 14.1 %fusion.1 = bf16[1,384,4096]{2,1,0:T(8,128)(2,1)} fusion(bf16[128,6,4096]{2,1,0:T(8,128)(2,1)} %reshape.156, f32[128,6]{0,1:T(8,128)S(1)} %copy.32, f32[128,1,6,384]{3,0,2,1:T(8,128)} %fusion.20, f32[128,1,6,384]{3,0,2,1:T(8,128)} %fusion.25), kind=kOutput, calls=%fused_computation.9 | convolution fusion | flops 2419556352 | bytes 11799552 | tf_op jit(solution)/shard_map/sech,secd->ehd/dot_general | solution.py:60
  429.2 3.5 gather_fusion.4
  433.4 77.6 %all-to-all-done.3 = bf16[128,6,2048]{2,1,0:T(8,128)(2,1)} async-done(((bf16[128,6,2048]{2,1,0:T(8,128)(2,1)}), bf16[128,6,2048]{2,1,0:T(8,128)(2,1)}, u32[]{:S(2)}, u32[]{:S(2)}) %all-to-all-start.3) | async-done | bytes 3145760 | tf_op jit(solution)/shard_map/all_to_all | solution.py:86
  511.0 6.3 %all_to_all.40 = bf16[768,2048]{1,0:T(8,128)(2,1)} reshape(bf16[128,6,2048]{2,1,0:T(8,128)(2,1)} %all-to-all-done.3) | data formatting | bytes 6291456 | tf_op jit(solution)/shard_map/all_to_all | solution.py:86
  517.4 7.6 %gather_fusion.3 = bf16[512,2048]{1,0:T(8,128)(2,1)} fusion(bf16[768,2048]{1,0:T(8,128)(2,1)} %all_to_all.40, s32[1024]{0:T(1024)S(1)} %pad_clamp_fusion), kind=kCustom, calls=%fused_computation.3 | custom fusion | bytes 4196352 | tf_op jit(solution)/shard_map/gather | solution.py:89
  524.9 3.7 bitcast_reduce_fusion
  (57 shorter events, 9.0 us)
Async XLA Ops:
  7.2 298.3 %copy-start = (bf16[1,4096,384]{2,1,0:T(8,128)(2,1)S(1)}, bf16[1,4096,384]{2,1,0:T(8,128)(2,1)}, u32[]{:S(2)}) copy-start(bf16[1,4096,384]{2,1,0:T(8,128)(2,1)} %param.11) | copy-start | bytes 9437188
  7.2 13.0 %copy-start.1 = (bf16[64,2048]{1,0:T(8,128)(2,1)S(1)}, bf16[64,2048]{1,0:T(8,128)(2,1)}, u32[]{:S(2)}) copy-start(bf16[64,2048]{1,0:T(8,128)(2,1)} %param.7) | copy-start | bytes 786436
  7.2 288.1 %all-gather.5.cloned.1.call-start = ((), (), s32[]{:S(2)}) async-start(), calls=%async_computation.7 | async-start | bytes 9437184 | tf_op jit(solution)/shard_map/all_gather | solution.py:43
  10.5 0.7 copy-start.7
  24.5 6.3 %copy-start.2 = (bf16[64,2048]{1,0:T(8,128)(2,1)S(1)}, bf16[64,2048]{1,0:T(8,128)(2,1)}, u32[]{:S(2)}) copy-start(bf16[64,2048]{1,0:T(8,128)(2,1)} %param.8) | copy-start | bytes 786436
  163.9 161.7 %all-gather.3.cloned.1.call-start = ((), (), s32[]{:S(2)}) async-start(), calls=%async_computation.6 | async-start | bytes 9437184 | tf_op jit(solution)/shard_map/all_gather | solution.py:44
  274.8 119.1 %reduce-scatter.2.cloned.1.call-start = ((), (), s32[]{:S(2)}) async-start(), calls=%async_computation.8 | async-start | bytes 9437184 | tf_op jit(solution)/shard_map/reduce_scatter | solution.py:78
  305.5 12.2 %copy-start.3 = (bf16[128,6,4096]{2,1,0:T(8,128)(2,1)S(1)}, bf16[128,6,4096]{2,1,0:T(8,128)(2,1)}, u32[]{:S(2)}) copy-start(bf16[128,6,4096]{2,1,0:T(8,128)(2,1)} %reshape.158) | copy-start | bytes 18874372
  305.5 12.2 %copy-start.5 = (bf16[1,4096,384]{2,1,0:T(8,128)(2,1)S(1)}, bf16[1,4096,384]{2,1,0:T(8,128)(2,1)}, u32[]{:S(2)}) copy-start(bf16[1,4096,384]{2,1,0:T(8,128)(2,1)} %param.12) | copy-start | bytes 9437188
  335.9 12.5 %copy-start.4 = (f32[128,1,6,384]{3,0,2,1:T(8,128)S(1)}, f32[128,1,6,384]{3,0,2,1:T(8,128)}, u32[]{:S(2)}) copy-start(f32[128,1,6,384]{3,0,2,1:T(8,128)} %fusion.25) | copy-start | bytes 3538948
  335.9 12.5 %copy-start.6 = (f32[128,1,6,384]{3,0,2,1:T(8,128)S(1)}, f32[128,1,6,384]{3,0,2,1:T(8,128)}, u32[]{:S(2)}) copy-start(f32[128,1,6,384]{3,0,2,1:T(8,128)} %fusion.20) | copy-start | bytes 3538948
  383.5 18.0 %all-to-all-start.4 = ((bf16[128,6,1]{1,2,0:T(2,128)(2,1)}), bf16[128,6,1]{1,2,0:T(2,128)(2,1)S(1)}, u32[]{:S(2)}, u32[]{:S(2)}) async-start(bf16[128,6,1]{1,2,0:T(2,128)(2,1)} %copy.37), calls=%async_computation.5 | async-start | bytes 131072 | tf_op jit(solution)/shard_map/all_to_all | solution.py:87
  401.4 109.6 %all-to-all-start.3 = ((bf16[128,6,2048]{2,1,0:T(8,128)(2,1)}), bf16[128,6,2048]{2,1,0:T(8,128)(2,1)}, u32[]{:S(2)}, u32[]{:S(2)}) async-start(bf16[128,6,2048]{2,1,0:T(8,128)(2,1)} %all_to_all.38), calls=%async_computation.4 | async-start | bytes 8388608 | tf_op jit(solution)/shard_map/all_to_all | solution.py:86
Sparse Core Ops, SparseCore 0:
  164.1 18.2 all-gather.4
  274.9 18.3 all-gather.2
  380.3 13.5 reduce-scatter.1
where the time goes:
time: 546 us; the launch traced here: 535 us
  blocking collectives  238 us (44%)
  local copies, waits for them, and re-layouts  107 us (20%)
  waiting for transfers between devices  82.7 us (15%)
  matrix products  61.5 us (11%)
  starting transfers between devices  20 us (4%)
  between operations  14.2 us (3%)
  other arithmetic  11.5 us (2%)
    all_to_all x1, blocking collectives, body(): lax.all_to_all(send_inputs, ('ex', 'ey'), split_axis=0, concat_axis=0, ti...  111 us
    all_to_all x1, blocking collectives, body(): lax.all_to_all(send_grads, ('ex', 'ey'), split_axis=0, concat_axis=0, til...  104 us
    all_to_all x1, waiting for transfers between devices, body(): lax.all_to_all(back_rows, ('ex', 'ey'), split_axis=0, concat_axis=0, tile...  77.6 us
    another operation x5, local copies, waits for them, and re-layouts  20.5 us
    all_to_all x1, blocking collectives, body(): lax.all_to_all(send_probs, ('ex', 'ey'), split_axis=0, concat_axis=0, til...  20.2 us
    convert_element_type x2, local copies, waits for them, and re-layouts, body(): partial_value.reshape(total_slots, width).astype(jnp.bfloat16)  16.9 us
    dot_general x1, matrix products, body(): jnp.einsum('sech,secd->ehd', weighted, rows_grad, preferred_element_type=...  14.1 us
    all_to_all x1, starting transfers between devices, body(): lax.all_to_all(back_rows, ('ex', 'ey'), split_axis=0, concat_axis=0, tile...  13.3 us
  transfers between devices with their start and end apart: 5, of which 3 were waited for; matrix products, arithmetic and copies ran while one was open for 9% of the time, Pallas kernels for 0%

commit v1 on v0

v1 whole, which is shorter than its diff:
```python
import jax
import jax.numpy as jnp
from jax import lax
from jax.sharding import PartitionSpec as P

LANES = 128


def dot(a, b, dims=((1,), (0,))):
    return lax.dot_general(a, b, (dims, ((), ())), preferred_element_type=jnp.float32)


def body(layer_input, out_grad, gate_prob, expert_ids, gate_weight, up_weight, down_weight):
    bf16, f32 = jnp.bfloat16, jnp.float32
    tok_rows, choose = expert_ids.shape
    half = layer_input.shape[1]
    hid = gate_weight.shape[2]
    n_high, n_low = lax.axis_size("ex"), lax.axis_size("ey")
    experts = n_high * n_low
    capacity = 3 * tok_rows * choose // (2 * experts) * n_high
    tokens = tok_rows * n_high
    slots = n_low * capacity
    high, low, core = lax.axis_index("ex"), lax.axis_index("ey"), lax.axis_index("tp")
    swap = [(0, 1), (1, 0)]

    own = core * half
    other = half - own
    gate_w, up_w, down_w = gate_weight[0], up_weight[0], down_weight[0]

    def in_order(w, axis):
        return (
            lax.dynamic_slice_in_dim(w, own, half, axis),
            lax.dynamic_slice_in_dim(w, other, half, axis),
        )

    both = jnp.concatenate([gate_w, up_w], axis=1)
    both_own, both_other = in_order(both, 0)
    down_own, down_other = in_order(down_w, 1)

    meta = jnp.concatenate(
        [
            expert_ids.astype(bf16),
            gate_prob,
            jnp.zeros((tok_rows, LANES - 2 * choose), bf16),
        ],
        axis=1,
    )
    packed = lax.all_gather(
        jnp.concatenate([layer_input, meta], axis=1), "ex", axis=0, tiled=True
    )
    all_grads = lax.all_gather(out_grad, "ex", axis=0, tiled=True)
    all_inputs = packed[:, :half]
    all_ids = packed[:, half : half + choose].astype(jnp.int32).T
    all_probs = packed[:, half + choose : half + 2 * choose].astype(f32).T

    mine = lax.broadcasted_iota(jnp.int32, (n_low, 1, 1), 0) + high * n_low
    named = all_ids[None, :, :] == mine
    chosen = jnp.sum(named.astype(f32), axis=1)
    weight = jnp.sum(jnp.where(named, all_probs[None], 0.0), axis=1)
    earlier = (
        lax.broadcasted_iota(jnp.int32, (tokens, tokens), 0)
        < lax.broadcasted_iota(jnp.int32, (tokens, tokens), 1)
    ).astype(bf16)
    rank = dot(chosen.astype(bf16), earlier).astype(jnp.int32)
    rank = jnp.where(chosen > 0, rank, -1)
    hit = rank[:, None, :] == lax.broadcasted_iota(jnp.int32, (1, capacity, 1), 1)
    pick = hit.astype(bf16).reshape(slots, tokens)
    pick_weighted = jnp.where(hit, weight[:, None, :], 0.0).astype(bf16).reshape(slots, tokens)

    def across(x):
        return lax.all_to_all(x, "ey", split_axis=0, concat_axis=0, tiled=True)

    rows_own = across(dot(pick, all_inputs).astype(bf16))
    rows_other = lax.ppermute(rows_own, "tp", swap)
    grads_own = across(dot(pick_weighted, all_grads).astype(bf16))
    grads_other = lax.ppermute(grads_own, "tp", swap)

    pre = dot(rows_own, both_own) + dot(rows_other, both_other)
    gate_pre, up_pre = pre[:, :hid], pre[:, hid:]
    gate_sigmoid = jax.nn.sigmoid(gate_pre)
    silu_gate = gate_pre * gate_sigmoid
    hidden_act = silu_gate * up_pre
    act = hidden_act.astype(bf16)

    hidden_grad = dot(grads_own, down_own, ((1,), (1,))) + dot(
        grads_other, down_other, ((1,), (1,))
    )
    prob_part = jnp.sum(hidden_grad * hidden_act, axis=1, keepdims=True)
    prob_total = prob_part + lax.ppermute(prob_part, "tp", swap)
    gate_grad = hidden_grad * up_pre * gate_sigmoid * (1.0 + gate_pre * (1.0 - gate_sigmoid))
    up_grad = hidden_grad * silu_gate
    grad_both = jnp.concatenate([gate_grad.astype(bf16), up_grad.astype(bf16)], axis=1)

    part_other = dot(grad_both, both_other, ((1,), (1,))).astype(bf16)
    part_here = lax.ppermute(part_other, "tp", swap)
    part_own = dot(grad_both, both_own, ((1,), (1,)))
    back = (part_own + part_here.astype(f32)).astype(bf16)
    lane = lax.broadcasted_iota(jnp.int32, (1, LANES), 1)
    back_probs = jnp.where(lane == high * n_low + low, prob_total, 0.0).astype(bf16)
    home = across(jnp.concatenate([back, back_probs], axis=1))

    grad_here = dot(act, grads_own, ((0,), (0,))).astype(bf16)
    grad_there = dot(act, grads_other, ((0,), (0,))).astype(bf16)
    first = core == 0
    down_grad = jnp.concatenate(
        [jnp.where(first, grad_here, grad_there), jnp.where(first, grad_there, grad_here)],
        axis=1,
    )

    sums = dot(pick, home, ((0,), (0,))).astype(bf16)
    final = lax.psum_scatter(sums, "ex", scatter_dimension=0, tiled=True)
    input_grad = final[:, :half]
    by_expert = final[:, half:].astype(f32)
    found = jnp.sum(
        jnp.where(expert_ids[:, :, None] == lane[None], by_expert[:, None, :], 0.0), axis=2
    )
    prob_grad = (found / gate_prob.astype(f32)).astype(bf16)
    return (input_grad, prob_grad, down_grad[None])


def solution(mesh):
    return jax.shard_map(
        body,
        mesh=mesh,
        in_specs=(
            P(("ex", "ey"), "tp"),
            P(("ex", "ey"), "tp"),
            P(("ex", "ey"), None),
            P(("ex", "ey"), None),
            P(("ex", "ey"), None, "tp"),
            P(("ex", "ey"), None, "tp"),
            P(("ex", "ey"), "tp", None),
        ),
        out_specs=(P(("ex", "ey"), "tp"), P(("ex", "ey"), None), P(("ex", "ey"), "tp", None)),
        check_vma=False,
    )
```

time: 546 us -> 290 us (0.53); the launches traced: 535 us -> 288 us
  blocking collectives: 238 us -> 46.1 us
  local copies, waits for them, and re-layouts: 107 us -> 6.69 us
  waiting for transfers between devices: 82.7 us -> 153 us
  matrix products: 61.5 us -> 48.2 us
  starting transfers between devices: 20 us -> 12.4 us
    all_to_all x3 -> x1, blocking collectives: 236 us -> 46.1 us  [across(): return lax.all_to_all(x, 'ey', split_axis=0, concat_axis=0, tiled=True)]
    all_gather x2, waiting for transfers between devices: 0.01 us -> 68.1 us  [the longest x1 43 us: body(): lax.all_gather(jnp.concatenate([layer_input, meta], axis=1), 'ex', axis=0...]
    gather x7 -> x0, local copies, waits for them, and re-layouts: 37.1 us -> none  [the longest x2 10.5 us: body(): layer_input[token_of]]
    all_to_all x2, waiting for transfers between devices: 78.8 us -> 49.6 us  [across(): return lax.all_to_all(x, 'ey', split_axis=0, concat_axis=0, tiled=True)]
    all_to_all x6 -> x0, local copies, waits for them, and re-layouts: 25.6 us -> none  [the longest x2 12.6 us: body(): lax.all_to_all(back_rows, ('ex', 'ey'), split_axis=0, concat_axis=0, tile...]
    reduce_scatter x1, waiting for transfers between devices: 3.86 us -> 29.2 us  [body(): final = lax.psum_scatter(sums, 'ex', scatter_dimension=0, tiled=True)]
    another operation x5 -> x0, local copies, waits for them, and re-layouts: 20.5 us -> none
    convert_element_type x4 -> x2, local copies, waits for them, and re-layouts: 17.8 us -> 0.19 us  [the longest x1 0.1 us: body(): expert_ids.astype(bf16)]
  transfers between devices with their start and end apart: 5 -> 9, of which waited for: 3 -> 7; matrix products, arithmetic and copies ran while one was open for 9% -> 13% of each run, Pallas kernels for 0% -> 0%
where the time goes in v1:
time: 290 us; the launch traced here: 288 us
  waiting for transfers between devices  153 us (53%)
  matrix products  48.2 us (17%)
  blocking collectives  46.1 us (16%)
  between operations  14 us (5%)
  starting transfers between devices  12.4 us (4%)
  other arithmetic  7.69 us (3%)
  local copies, waits for them, and re-layouts  6.69 us (2%)
    all_to_all x2, waiting for transfers between devices, across(): return lax.all_to_all(x, 'ey', split_axis=0, concat_axis=0, tiled=True)  49.6 us
    dot_general x12, matrix products, dot(): lax.dot_general(a, b, (dims, ((), ())), preferred_element_type=jnp.float32)  48.2 us
    all_to_all x1, blocking collectives, across(): return lax.all_to_all(x, 'ey', split_axis=0, concat_axis=0, tiled=True)  46.1 us
    all_gather x1, waiting for transfers between devices, body(): lax.all_gather(jnp.concatenate([layer_input, meta], axis=1), 'ex', axis=0...  43 us
    reduce_scatter x1, waiting for transfers between devices, body(): final = lax.psum_scatter(sums, 'ex', scatter_dimension=0, tiled=True)  29.2 us
    all_gather x1, waiting for transfers between devices, body(): all_grads = lax.all_gather(out_grad, 'ex', axis=0, tiled=True)  25 us
    all_to_all x2, starting transfers between devices, across(): return lax.all_to_all(x, 'ey', split_axis=0, concat_axis=0, tiled=True)  11.3 us
  transfers between devices with their start and end apart: 9, of which 7 were waited for; matrix products, arithmetic and copies ran while one was open for 13% of the time, Pallas kernels for 0%

profile of v1, /device:TPU:32, one launch (start us, length us, event | category | flops | bytes accessed | tf_op | source)
XLA Modules:
  0.0 287.8 jit_solution(15093202147309162890)
XLA Ops:
  7.2 0.8 convert_element_type.65
  8.2 0.8 copy.21
  9.0 1.7 concatenate.15
  10.8 0.7 all-gather.5.cloned.1.call-update
  11.6 43.0 %all-gather.3.cloned.1.call-done = bf16[512,2176]{1,0:T(8,128)(2,1)} async-done(((bf16[64,2176]{1,0:T(8,128)(2,1)}), bf16[512,2176]{1,0:T(8,128)(2,1)}) %all-gather.3.cloned.1.call-update) | async-done | bytes 2228240 | tf_op jit(solution)/shard_map/all_gather | solution.py:48
  54.6 1.8 convert_bitcast_fusion
  56.4 1.0 copy.22
  58.2 5.1 %convolution_convert_fusion.2 = bf16[768,2048]{1,0:T(8,128)(2,1)} fusion(pred[768,512]{1,0:T(32,128)(4,1)S(1)} %bitcast_compare_fusion, bf16[512,2176]{1,0:T(8,128)(2,1)} %all-gather.3.cloned.1.call-done), kind=kOutput, calls=%fused_computation.9 | convolution fusion | flops 1612185600 | bytes 5636096 | tf_op jit(solution)/shard_map/dot_general | solution.py:10
  63.3 6.9 %all-to-all-start.1 = ((bf16[16,48,2048]{2,1,0:T(8,128)(2,1)}), bf16[16,48,2048]{2,1,0:T(8,128)(2,1)}, u32[]{:S(2)}, u32[]{:S(2)}) async-start(bf16[16,48,2048]{2,1,0:T(8,128)(2,1)} %bitcast.49), calls=%async_computation.1 | async-start | bytes 6291456 | tf_op jit(solution)/shard_map/all_to_all | solution.py:71
  70.1 1.1 fusion.8
  71.2 25.0 %all-gather.5.cloned.1.call-done = bf16[512,2048]{1,0:T(8,128)(2,1)} async-done(((bf16[64,2048]{1,0:T(8,128)(2,1)}), bf16[512,2048]{1,0:T(8,128)(2,1)}) %all-gather.5.cloned.1.call-update) | async-done | bytes 2097168 | tf_op jit(solution)/shard_map/all_gather | solution.py:51
  96.3 5.3 %convolution_convert_fusion = bf16[768,2048]{1,0:T(8,128)(2,1)} fusion(bf16[768,512]{1,0:T(8,128)(2,1)} %fusion.8, bf16[512,2048]{1,0:T(8,128)(2,1)} %all-gather.5.cloned.1.call-done), kind=kOutput, calls=%fused_computation.7 | convolution fusion | flops 1612185600 | bytes 6029312 | tf_op jit(solution)/shard_map/dot_general | solution.py:10
  101.6 7.0 %all-to-all-done.1 = bf16[16,48,2048]{2,1,0:T(8,128)(2,1)} async-done(((bf16[16,48,2048]{2,1,0:T(8,128)(2,1)}), bf16[16,48,2048]{2,1,0:T(8,128)(2,1)}, u32[]{:S(2)}, u32[]{:S(2)}) %all-to-all-start.1) | async-done | bytes 3145760 | tf_op jit(solution)/shard_map/all_to_all | solution.py:71
  108.6 4.5 %all-to-all-start = ((bf16[16,48,2048]{2,1,0:T(8,128)(2,1)}), bf16[16,48,2048]{2,1,0:T(8,128)(2,1)}, u32[]{:S(2)}, u32[]{:S(2)}) async-start(bf16[16,48,2048]{2,1,0:T(8,128)(2,1)} %bitcast.48), calls=%async_computation | async-start | bytes 6291456 | tf_op jit(solution)/shard_map/all_to_all | solution.py:71
  113.2 42.7 %all-to-all-done = bf16[16,48,2048]{2,1,0:T(8,128)(2,1)} async-done(((bf16[16,48,2048]{2,1,0:T(8,128)(2,1)}), bf16[16,48,2048]{2,1,0:T(8,128)(2,1)}, u32[]{:S(2)}, u32[]{:S(2)}) %all-to-all-start) | async-done | bytes 3145760 | tf_op jit(solution)/shard_map/all_to_all | solution.py:71
  155.9 3.5 %fusion.6 = f32[768,384]{0,1:T(8,128)S(1)} fusion(bf16[768,2048]{1,0:T(8,128)(2,1)} %bitcast.5, bf16[1,384,4096]{2,1,0:T(8,128)(2,1)S(1)} %copy-done, s32[]{:T(128)S(6)} %select_n.44), kind=kOutput, calls=%fused_computation.19 | convolution fusion | flops 1207959552 | bytes 5898244 | tf_op jit(solution)/shard_map/dot_general | solution.py:10
  159.7 4.7 %fusion.29 = f32[768,768]{0,1:T(8,128)S(1)} fusion(bf16[768,2048]{1,0:T(8,128)(2,1)} %bitcast.9, s32[]{:T(128)S(6)} %select_n.44, bf16[4096,384]{1,0:T(8,128)(2,1)S(1)} %bitcast.51, bf16[4096,384]{1,0:T(8,128)(2,1)S(1)} %bitcast.55), kind=kOutput, calls=%fused_computation.63 | convolution fusion | flops 2422210560 | bytes 11796484 | tf_op jit(solution)/shard_map/dot_general | solution.py:10
  164.4 4.8 %convolution_add_fusion = f32[768,768]{0,1:T(8,128)S(1)} fusion(f32[768,768]{0,1:T(8,128)S(1)} %fusion.29, bf16[768,2048]{1,0:T(8,128)(2,1)} %collective-permute-done.1, s32[]{:T(128)S(6)} %select_n.45, bf16[4096,384]{1,0:T(8,128)(2,1)S(1)} %bitcast.52, bf16[4096,384]{1,0:T(8,128)(2,1)S(1)} %bitcast.56), kind=kOutput, calls=%fused_computation.29 | convolution fusion | flops 2422800384 | bytes 14155780 | tf_op jit(solution)/shard_map/dot_general | solution.py:10
  169.2 4.7 %multiply_convert_fusion.1 = (bf16[768,384]{0,1:T(8,128)(2,1)S(1)}, f32[768]{0:T(1024)S(1)}, bf16[768,384]{0,1:T(8,128)(2,1)S(1)}, bf16[768,384]{0,1:T(8,128)(2,1)}) fusion(f32[768,768]{0,1:T(8,128)S(1)} %convolution_add_fusion, f32[768,384]{0,1:T(8,128)S(1)} %fusion.6, bf16[768,2048]{1,0:T(8,128)(2,1)} %collective-permute-done, ...), kind=kOutput, calls=%fused_computation.34 | convolution fusion | flops 1213267200 | bytes 10030084 | tf_op jit(solution)/shard_map/dot_general | solution.py:10
  173.9 4.0 %convolution_convert_fusion.1 = bf16[768,2048]{1,0:T(8,128)(2,1)} fusion(bf16[768,384]{0,1:T(8,128)(2,1)S(1)} %get-tuple-element.10, bf16[768,384]{0,1:T(8,128)(2,1)S(1)} %get-tuple-element.8, s32[]{:T(128)S(6)} %select_n.45, bf16[4096,384]{1,0:T(8,128)(2,1)S(1)} %bitcast.53, bf16[4096,384]{1,0:T(8,128)(2,1)S(1)} %bitcast.57), kind=kOutput, calls=%fused_computation.8 | convolution fusion | flops 2426142720 | bytes 10616836 | tf_op jit(solution)/shard_map/dot_general | solution.py:10
  178.0 0.5 collective-permute-start.2
  178.8 4.8 %collective-permute-done.3 = f32[768,1]{0,1:T(1,128)S(1)} collective-permute-done((f32[768,1]{0,1:T(1,128)S(1)}, f32[768,1]{0,1:T(1,128)S(1)}, u32[]{:S(2)}, u32[]{:S(2)}) %collective-permute-start.3) | collective-permute-done | bytes 3104 | tf_op jit(solution)/shard_map/ppermute | solution.py:89
  184.1 5.9 %add_convert_fusion = bf16[768,2048]{1,0:T(8,128)(2,1)S(1)} fusion(bf16[768,2048]{1,0:T(8,128)(2,1)} %collective-permute-done.2, bf16[768,384]{0,1:T(8,128)(2,1)} %copy-done.8, bf16[768,384]{0,1:T(8,128)(2,1)} %copy-done.7, s32[]{:T(128)S(6)} %select_n.44, bf16[4096,384]{1,0:T(8,128)(2,1)} %bitcast.50, bf16[4096,384]{1,0:T(8,128)(2,1)} %bitcast.54), kind=kOutput, calls=%fused_computation.4 | convolution fusion | flops 2429288448 | bytes 13762564 | tf_op jit(solution)/shard_map/dot_general | solution.py:10
  190.3 46.1 %all_to_all.33 = bf16[16,48,2176]{2,1,0:T(8,128)(2,1)S(1)} all-to-all(bf16[16,48,2176]{2,1,0:T(8,128)(2,1)S(1)} %bitcast.47), channel_id=1, replica_groups=mesh['ex'=8,'ey'=16,'tp'=2] {'ey'}, dimensions={0} | all-to-all | bytes 6684672 | tf_op jit(solution)/shard_map/all_to_all | solution.py:71
  236.4 3.5 %fusion = bf16[512,2176]{1,0:T(8,128)(2,1)} fusion(bf16[16,48,2176]{2,1,0:T(8,128)(2,1)S(1)} %all_to_all.33, s32[16,512]{1,0:T(8,128)S(1)} %fusion.15), kind=kOutput, calls=%fused_computation.6 | convolution fusion | flops 1712783360 | bytes 5603328 | tf_op jit(solution)/shard_map/dot_general | solution.py:10
  240.1 3.3 %convolution_convert_fusion.4 = bf16[384,2048]{1,0:T(8,128)(2,1)S(1)} fusion(bf16[768,384]{0,1:T(8,128)(2,1)S(1)} %copy-done.6, bf16[768,2048]{1,0:T(8,128)(2,1)} %bitcast.5), kind=kOutput, calls=%fused_computation.15 | convolution fusion | flops 1208745984 | bytes 5308416 | tf_op jit(solution)/shard_map/dot_general | solution.py:10
  243.4 3.3 %broadcast_select_fusion.1 = (bf16[384,2048]{1,0:T(8,128)(2,1)S(1)}, bf16[384,2048]{1,0:T(8,128)(2,1)S(1)}) fusion(bf16[384,2048]{1,0:T(8,128)(2,1)S(1)} %convolution_convert_fusion.4, pred[]{:T(512)S(6)} %eq.81, bf16[768,384]{0,1:T(8,128)(2,1)S(1)} %copy-done.6, bf16[768,2048]{1,0:T(8,128)(2,1)} %collective-permute-done), kind=kOutput, calls=%fused_computation.28 | convolution fusion | flops 1210318848 | bytes 8454145 | tf_op jit(solution)/shard_map/dot_general | solution.py:10
  246.7 2.0 maximum_bitcast_fusion
  248.7 29.2 %reduce-scatter.2.cloned.1.call-done = bf16[64,2176]{1,0:T(8,128)(2,1)} async-done(((bf16[512,2176]{1,0:T(8,128)(2,1)}), bf16[64,2176]{1,0:T(8,128)(2,1)}) %reduce-scatter.2.cloned.1.call-update) | async-done | bytes 278544 | tf_op jit(solution)/shard_map/reduce_scatter | solution.py:111
  278.0 0.7 slice_convert_fusion
  279.0 0.7 copy.26
  279.6 1.7 slice.33
  (47 shorter events, 3.1 us)
Async XLA Ops:
  7.2 148.7 %copy-start = (bf16[1,384,4096]{2,1,0:T(8,128)(2,1)S(1)}, bf16[1,384,4096]{2,1,0:T(8,128)(2,1)}, u32[]{:S(2)}) copy-start(bf16[1,384,4096]{2,1,0:T(8,128)(2,1)} %param.13) | copy-start | bytes 9437188
  7.2 47.4 %all-gather.3.cloned.1.call-start = ((), (), s32[]{:S(2)}) async-start(), calls=%async_computation.4 | async-start | bytes 2506752 | tf_op jit(solution)/shard_map/all_gather | solution.py:48
  10.7 85.5 %all-gather.5.cloned.1.call-start = ((), (), s32[]{:S(2)}) async-start(), calls=%async_computation.5 | async-start | bytes 2359296 | tf_op jit(solution)/shard_map/all_gather | solution.py:51
  63.3 45.3 %all-to-all-start.1 = ((bf16[16,48,2048]{2,1,0:T(8,128)(2,1)}), bf16[16,48,2048]{2,1,0:T(8,128)(2,1)}, u32[]{:S(2)}, u32[]{:S(2)}) async-start(bf16[16,48,2048]{2,1,0:T(8,128)(2,1)} %bitcast.49), calls=%async_computation.1 | async-start | bytes 6291456 | tf_op jit(solution)/shard_map/all_to_all | solution.py:71
  108.6 47.3 %all-to-all-start = ((bf16[16,48,2048]{2,1,0:T(8,128)(2,1)}), bf16[16,48,2048]{2,1,0:T(8,128)(2,1)}, u32[]{:S(2)}, u32[]{:S(2)}) async-start(bf16[16,48,2048]{2,1,0:T(8,128)(2,1)} %bitcast.48), calls=%async_computation | async-start | bytes 6291456 | tf_op jit(solution)/shard_map/all_to_all | solution.py:71
  113.1 164.9 %reduce-scatter.2.cloned.1.call-start = ((), (), s32[]{:S(2)}) async-start(), calls=%async_computation.6 | async-start | bytes 2506752 | tf_op jit(solution)/shard_map/reduce_scatter | solution.py:111
  113.1 51.3 %collective-permute-start.1 = (bf16[768,2048]{1,0:T(8,128)(2,1)}, bf16[768,2048]{1,0:T(8,128)(2,1)}, u32[]{:S(2)}, u32[]{:S(2)}) collective-permute-start(bf16[768,2048]{1,0:T(8,128)(2,1)} %bitcast.9), channel_id=1, source_target_pairs={{0,1},{1,0},{2,3},{3,2},{4,5},{5,4},{6,7},{7,6},{8,9},{9,8},{10,11... | collective-permute-start | bytes 9437192 | tf_op jit(solution)/shard_map/ppermute | solution.py:74
  155.9 13.4 %collective-permute-start = (bf16[768,2048]{1,0:T(8,128)(2,1)}, bf16[768,2048]{1,0:T(8,128)(2,1)}, u32[]{:S(2)}, u32[]{:S(2)}) collective-permute-start(bf16[768,2048]{1,0:T(8,128)(2,1)} %bitcast.5), channel_id=1, source_target_pairs={{0,1},{1,0},{2,3},{3,2},{4,5},{5,4},{6,7},{7,6},{8,9},{9,8},{10,11... | collective-permute-start | bytes 9437192 | tf_op jit(solution)/shard_map/ppermute | solution.py:76
  155.9 3.5 %copy-start.4 = (bf16[1,4096,384]{2,1,0:T(8,128)(2,1)S(1)}, bf16[1,4096,384]{2,1,0:T(8,128)(2,1)}, u32[]{:S(2)}) copy-start(bf16[1,4096,384]{2,1,0:T(8,128)(2,1)} %param.11) | copy-start | bytes 9437188
  155.9 3.8 %copy-start.5 = (bf16[1,4096,384]{2,1,0:T(8,128)(2,1)S(1)}, bf16[1,4096,384]{2,1,0:T(8,128)(2,1)}, u32[]{:S(2)}) copy-start(bf16[1,4096,384]{2,1,0:T(8,128)(2,1)} %param.12) | copy-start | bytes 9437188
  173.9 4.0 %copy-start.7 = (bf16[768,384]{0,1:T(8,128)(2,1)}, bf16[768,384]{0,1:T(8,128)(2,1)S(1)}, u32[]{:S(2)}) copy-start(bf16[768,384]{0,1:T(8,128)(2,1)S(1)} %get-tuple-element.8) | copy-start | bytes 1769476
  173.9 4.0 %copy-start.8 = (bf16[768,384]{0,1:T(8,128)(2,1)}, bf16[768,384]{0,1:T(8,128)(2,1)S(1)}, u32[]{:S(2)}) copy-start(bf16[768,384]{0,1:T(8,128)(2,1)S(1)} %get-tuple-element.10) | copy-start | bytes 1769476
  178.0 6.1 %collective-permute-start.2 = (bf16[768,2048]{1,0:T(8,128)(2,1)}, bf16[768,2048]{1,0:T(8,128)(2,1)}, u32[]{:S(2)}, u32[]{:S(2)}) collective-permute-start(bf16[768,2048]{1,0:T(8,128)(2,1)} %convolution_convert_fusion.1), channel_id=1, source_target_pairs={{0,1},{1,0},{2,3},{3,2},{4,5},{5,4},{6,7},{7,6},{8,9},{9,8},{10,11... | collective-permute-start | bytes 9437192 | tf_op jit(solution)/shard_map/ppermute | solution.py:95
  178.5 5.2 %collective-permute-start.3 = (f32[768,1]{0,1:T(1,128)S(1)}, f32[768,1]{0,1:T(1,128)S(1)}, u32[]{:S(2)}, u32[]{:S(2)}) collective-permute-start(f32[768,1]{0,1:T(1,128)S(1)} %broadcast_in_dim.87), channel_id=1, source_target_pairs={{0,1},{1,0},{2,3},{3,2},{4,5},{5,4},{6,7},{7,6},{8,9},{9,8},{10,11... | collective-permute-start | bytes 9224 | tf_op jit(solution)/shard_map/ppermute | solution.py:89
  236.4 3.5 %copy-start.2 = (s32[64,8]{0,1:T(8,128)S(1)}, s32[64,8]{0,1:T(8,128)}, u32[]{:S(2)}) copy-start(s32[64,8]{0,1:T(8,128)} %param.10) | copy-start | bytes 6148
  236.4 3.6 %copy-start.3 = (bf16[64,8]{0,1:T(8,128)(2,1)S(1)}, bf16[64,8]{0,1:T(8,128)(2,1)}, u32[]{:S(2)}) copy-start(bf16[64,8]{0,1:T(8,128)(2,1)} %param.9) | copy-start | bytes 3076
  236.4 3.7 %copy-start.6 = (bf16[768,384]{0,1:T(8,128)(2,1)S(1)}, bf16[768,384]{0,1:T(8,128)(2,1)}, u32[]{:S(2)}) copy-start(bf16[768,384]{0,1:T(8,128)(2,1)} %get-tuple-element.13) | copy-start | bytes 1769476
  246.7 34.6 %copy-start.1 = (bf16[1,384,4096]{2,1,0:T(8,128)(2,1)S(1)}, bf16[1,384,4096]{2,1,0:T(8,128)(2,1)}, u32[]{:S(2)}) copy-start(bf16[1,384,4096]{2,1,0:T(8,128)(2,1)} %param.13) | copy-start | bytes 9437188
Sparse Core Ops, SparseCore 0:
  10.8 43.7 all-gather.2
  56.4 39.8 all-gather.4
  240.1 37.8 reduce-scatter.1
